TPU v7x, 32 devices: a whole 2x2x4 slice. The times are simulated.
32 devices in a mesh: ctx: 16 (over z, y, core), tp: 2 (over x).
Axes of the slice: x: 2, y: 2, z: 4, core: 2. Of those that a mesh axis runs over, the one named last changes fastest.
Arguments:
- tokens: bfloat16 [1024, 8192], P('tp', 'ctx'), may hold values from -6 to 6
- w_in: bfloat16 [8192, 24576], P('tp', 'ctx'), may hold values from -0.0625 to 0.0625
- short_taps: float32 [3, 24576], P(None, ('ctx', 'tp')), may hold values from -1 to 1
- li_residue: float32 [8192, 16], P(('ctx', 'tp')), may hold values from -0.5 to 0.5
- li_rate: float32 [8192, 16], P(('ctx', 'tp')), may hold values from 0.00048828125 to 0.1
- cotangent: bfloat16 [8192, 1024], P(('ctx', 'tp')), may hold values from -6 to 6
Outputs:
- mixed: bfloat16 [8192, 1024], P(('ctx', 'tp'))
- grad_tokens: bfloat16 [8192, 1024], P('ctx', 'tp')
All inputs are finite; a program needn't handle non-finite values.
Results may differ from a plain program's by a relative error of at most 0.014.
Values may be sent and summed in bfloat16 or wider, within the bound.
A program may use at most 192 MiB of HBM per device.

v0:
```python
import math

import jax
import jax.numpy as jnp
from jax import lax
from jax.sharding import PartitionSpec as P

HIGH = lax.Precision.HIGHEST


def causal_taps(signal, taps):
    seq_len = signal.shape[0]
    features = signal * taps[0]
    for delay in range(1, taps.shape[0]):
        shifted = jnp.concatenate(
            [jnp.zeros((delay, signal.shape[1]), signal.dtype), signal[: seq_len - delay]], axis=0
        )
        features = features + shifted * taps[delay]
    return features


def long_filter(signal, residue, decay):
    chan_count, seq_len = signal.shape
    tile_size = math.gcd(seq_len, 128)
    tile_count = seq_len // tile_size
    tiled = signal.reshape(chan_count, tile_count, tile_size)
    offsets = jnp.arange(tile_size, dtype=jnp.float32)
    head_taps = jnp.einsum(
        "cm,cml->cl", residue, jnp.exp(-decay[:, :, None] * offsets[None, None, :]), precision=HIGH
    )
    distance = jnp.arange(tile_size)[:, None] - jnp.arange(tile_size)[None, :]
    clipped = jnp.maximum(distance, 0)
    current = jnp.where(distance >= 0, head_taps[:, clipped], 0.0)
    inside = jnp.einsum("cts,cbs->cbt", current, tiled, precision=HIGH)
    end_decay = jnp.exp(-decay[:, :, None] * (tile_size - 1.0 - offsets)[None, None, :])
    states = jnp.einsum("cbt,cmt->cmb", tiled, end_decay, precision=HIGH)
    tile_index = jnp.arange(tile_count)
    tile_gap = tile_index[:, None] - 1 - tile_index[None, :]
    spans = (tile_size * jnp.maximum(tile_gap, 0)).astype(jnp.float32)
    carry_weight = jnp.where(tile_gap >= 0, jnp.exp(-decay[:, :, None, None] * spans), 0.0)
    carried = jnp.einsum("cmbk,cmk->cmb", carry_weight, states, precision=HIGH)
    start_decay = jnp.exp(-decay[:, :, None] * (offsets + 1.0)[None, None, :])
    across = jnp.einsum("cm,cmb,cmt->cbt", residue, carried, start_decay, precision=HIGH)
    return (inside + across).reshape(chan_count, seq_len)


def mixer(signal, taps, residue, decay):
    seq_len = signal.shape[0]
    chan_count = residue.shape[0]
    features = causal_taps(signal, taps).reshape(seq_len, chan_count, 3)
    query_part = features[:, :, 0].T
    key_part = features[:, :, 1].T
    value_part = features[:, :, 2].T
    return query_part * long_filter(key_part * value_part, residue, decay)


def shards(tokens, w_in, short_taps, li_residue, li_rate, cotangent):
    features = lax.all_gather(tokens, "ctx", axis=1, tiled=True)
    weights = lax.all_gather(w_in, "tp", axis=0, tiled=True)
    projected = jnp.dot(features, weights, preferred_element_type=jnp.float32)
    rounded = projected.astype(jnp.bfloat16)
    channels = lax.all_to_all(rounded, "tp", split_axis=1, concat_axis=0, tiled=True)
    signal = channels.astype(jnp.float32)

    def local_mix(given):
        return mixer(given, short_taps, li_residue, li_rate)

    mixed_out, pullback = jax.vjp(local_mix, signal)
    grad_signal = pullback(cotangent.astype(jnp.float32))[0]
    grad_rounded = grad_signal.astype(jnp.bfloat16)
    grad_rows = lax.all_to_all(grad_rounded, "tp", split_axis=0, concat_axis=1, tiled=True)
    summed = lax.psum_scatter(
        lax.dot_general(
            weights, grad_rows, (((1,), (1,)), ((), ())), preferred_element_type=jnp.float32
        ).astype(jnp.bfloat16),
        "ctx",
        scatter_dimension=0,
        tiled=True,
    )
    return (mixed_out.astype(jnp.bfloat16), summed)


def solution(mesh):
    in_specs = (
        P("tp", "ctx"),
        P("tp", "ctx"),
        P(None, ("ctx", "tp")),
        P(("ctx", "tp"), None),
        P(("ctx", "tp"), None),
        P(("ctx", "tp"), None),
    )
    out_specs = (P(("ctx", "tp"), None), P("ctx", "tp"))
    return jax.shard_map(shards, mesh=mesh, in_specs=in_specs, out_specs=out_specs, check_vma=False)
```

profile of v0, /device:TPU:2, one launch (start us, length us, event | category | flops | bytes accessed | tf_op | source)
XLA Modules:
  0.0 685.8 jit_solution(18406063462156226287)
XLA Ops:
  11.2 62.0 %gather_fusion = f32[16384,256]{1,0:T(8,128)} fusion(f32[256,128]{0,1:T(8,128)S(1)} %copy.43, s32[16384]{0:T(1024)S(1)} %bitcast_clamp_fusion), kind=kCustom, calls=%fused_computation | custom fusion | bytes 33619968 | tf_op jit(solution)/shard_map/jvp()/gather | solution.py:33
  73.2 18.2 %copy.32 = f32[128,128,256]{1,0,2:T(8,128)} copy(f32[128,128,256]{2,1,0:T(8,128)} %bitcast.96) | data formatting | bytes 33554432 | tf_op jit(solution)/shard_map/jvp()/gather | solution.py:33
  91.4 290.4 %all-gather.5.cloned.1.call-done = bf16[8192,1536]{1,0:T(8,128)(2,1)} async-done(((bf16[4096,1536]{1,0:T(8,128)(2,1)}), bf16[8192,1536]{1,0:T(8,128)(2,1)}) %all-gather.5.cloned.1.call-update) | async-done | bytes 25165840 | tf_op jit(solution)/shard_map/all_gather | solution.py:59
  381.8 19.3 %convolution_convert_fusion.1 = bf16[512,1536]{1,0:T(8,128)(2,1)S(1)} fusion(bf16[512,8192]{1,0:T(8,128)(2,1)} %all-gather.3.cloned.1.call-done, bf16[8192,1536]{1,0:T(8,128)(2,1)} %all-gather.5.cloned.1.call-done), kind=kOutput, calls=%fused_computation.18 | convolution fusion | flops 12885688320 | bytes 35127296 | tf_op jit(solution)/shard_map/dot_general | solution.py:60
  402.4 5.4 all-to-all-start
  409.7 15.8 %all-to-all-done = bf16[512,2,768]{2,0,1:T(8,128)(2,1)S(1)} async-done(((bf16[512,2,768]{2,0,1:T(8,128)(2,1)}), bf16[512,2,768]{2,0,1:T(8,128)(2,1)S(1)}, u32[]{:S(2)}, u32[]{:S(2)}) %all-to-all-start) | async-done | bytes 1572896 | tf_op jit(solution)/shard_map/all_to_all | solution.py:62
  425.8 2.7 multiply_add_fusion
  428.5 2.5 copy.28
  431.0 3.0 reshape.88
  434.1 9.2 %fusion.37 = (f32[1024,256,1]{0,2,1:T(1,128)}, f32[1024,256,1]{0,2,1:T(1,128)S(1)}, f32[1024,256,1]{0,2,1:T(1,128)}) fusion(f32[1024,256,3]{0,2,1:T(4,128)} %reshape.88), kind=kLoop, calls=%fused_computation.70 | loop fusion | bytes 6291456 | tf_op jit(solution)/shard_map/jvp()/slice | solution.py:53
  443.8 3.5 fusion.17
  450.7 17.2 %fusion = f32[256,8,128]{2,1,0:T(8,128)S(1)} fusion(f32[256,8,128]{2,1,0:T(8,128)S(1)} %bitcast.100, f32[128,128,256]{1,0,2:T(8,128)} %copy.32, pred[128,128]{1,0:T(8,128)(4,1)S(1)} %subtract_compare_fusion), kind=kOutput, calls=%fused_computation.1 | convolution fusion | flops 406847488 | bytes 18890752 | tf_op jit(solution)/shard_map/transpose(jvp(cts,cbs->cbt))/dot_general | solution.py:34
  468.0 2.1 fusion.15
  472.7 27.7 %fusion.2 = f32[256,8,128]{2,1,0:T(8,128)} fusion(f32[256,8,128]{2,1,0:T(8,128)S(1)} %bitcast.101, f32[128,128,256]{1,0,2:T(8,128)S(1)} %bitcast.95, pred[128,128]{1,0:T(8,128)(4,1)S(1)} %subtract_compare_fusion), kind=kOutput, calls=%fused_computation.3 | convolution fusion | flops 406847488 | bytes 18890752 | tf_op jit(solution)/shard_map/jvp(cts,cbs->cbt)/dot_general | solution.py:34
  500.5 3.6 fusion.14
  507.6 3.6 fusion.16
  512.8 4.1 copy.34
  516.9 5.9 reshape.93
  522.8 2.5 copy.35
  526.8 2.1 add_convert_fusion
  530.6 21.1 %all_to_all.32 = bf16[2,512,768]{1,2,0:T(8,128)(2,1)S(1)} all-to-all(bf16[2,512,768]{1,2,0:T(8,128)(2,1)S(1)} %copy.38), channel_id=1, replica_groups=mesh['ctx'=16,'tp'=2] {'tp'}, dimensions={0} | all-to-all | bytes 3145728 | tf_op jit(solution)/shard_map/all_to_all | solution.py:71
  551.7 19.1 %fusion.6 = bf16[8192,512]{0,1:T(8,128)(2,1)} fusion(bf16[512,1536]{0,1:T(8,128)(2,1)S(1)} %bitcast.106, bf16[8192,1536]{1,0:T(8,128)(2,1)} %all-gather.5.cloned.1.call-done), kind=kOutput, calls=%fused_computation.8 | convolution fusion | flops 12889096192 | bytes 35127296 | tf_op jit(solution)/shard_map/dot_general | solution.py:73
  570.9 106.2 %reduce-scatter.2.cloned.1.call-done = bf16[512,512]{0,1:T(8,128)(2,1)} async-done(((bf16[8192,512]{0,1:T(8,128)(2,1)}), bf16[512,512]{0,1:T(8,128)(2,1)}) %reduce-scatter.2.cloned.1.call-update) | async-done | bytes 524304 | tf_op jit(solution)/shard_map/reduce_scatter | solution.py:72
  677.1 2.0 copy.39
  (82 shorter events, 21.9 us)
Async XLA Ops:
  7.2 84.2 %all-gather.3.cloned.1.call-start = ((), (), s32[]{:S(2)}) async-start(), calls=%async_computation.3 | async-start | bytes 8912896 | tf_op jit(solution)/shard_map/all_gather | solution.py:58
  7.9 0.8 copy-start.13
  7.9 0.9 copy-start.14
  7.9 373.9 %all-gather.5.cloned.1.call-start = ((), (), s32[]{:S(2)}) async-start(), calls=%async_computation.4 | async-start | bytes 37748736 | tf_op jit(solution)/shard_map/all_gather | solution.py:59
  91.4 352.4 %copy-start.16 = (f32[128]{0:T(128)}, f32[128]{0:T(128)S(1)}, u32[]{:S(2)}) copy-start(f32[128]{0:T(128)S(1)} %iota_add_fusion) | copy-start | bytes 1540
  401.1 7.2 %copy-start.15 = (f32[3,768]{1,0:T(4,128)S(1)}, f32[3,768]{1,0:T(4,128)}, u32[]{:S(2)}) copy-start(f32[3,768]{1,0:T(4,128)} %param.8) | copy-start | bytes 27652
  402.4 23.1 %all-to-all-start = ((bf16[512,2,768]{2,0,1:T(8,128)(2,1)}), bf16[512,2,768]{2,0,1:T(8,128)(2,1)S(1)}, u32[]{:S(2)}, u32[]{:S(2)}) async-start(bf16[512,2,768]{2,0,1:T(8,128)(2,1)} %bitcast.91), calls=%async_computation | async-start | bytes 3145728 | tf_op jit(solution)/shard_map/all_to_all | solution.py:62
  407.8 269.3 %reduce-scatter.2.cloned.1.call-start = ((), (), s32[]{:S(2)}) async-start(), calls=%async_computation.5 | async-start | bytes 8912896 | tf_op jit(solution)/shard_map/reduce_scatter | solution.py:72
  408.3 17.4 %copy-start.7 = (f32[768]{0:T(1024)}, f32[768]{0:T(1024)S(1)}, u32[]{:S(2)}) copy-start(f32[768]{0:T(1024)S(1)} %get-tuple-element.8) | copy-start | bytes 9220
  408.3 17.4 %copy-start.9 = (f32[768]{0:T(1024)}, f32[768]{0:T(1024)S(1)}, u32[]{:S(2)}) copy-start(f32[768]{0:T(1024)S(1)} %get-tuple-element.9) | copy-start | bytes 9220
  408.3 17.4 %copy-start.11 = (f32[768]{0:T(1024)}, f32[768]{0:T(1024)S(1)}, u32[]{:S(2)}) copy-start(f32[768]{0:T(1024)S(1)} %get-tuple-element.10) | copy-start | bytes 9220
  434.1 9.2 %copy-start.3 = (bf16[256,1024]{1,0:T(8,128)(2,1)S(1)}, bf16[256,1024]{1,0:T(8,128)(2,1)}, u32[]{:S(2)}) copy-start(bf16[256,1024]{1,0:T(8,128)(2,1)} %param.11) | copy-start | bytes 1572868
  450.7 17.3 %copy-start.17 = (f32[128]{0:T(128)S(1)}, f32[128]{0:T(128)}, u32[]{:S(2)}) copy-start(f32[128]{0:T(128)} %iota_subtract_fusion.1) | copy-start | bytes 1540
  450.7 21.4 %slice-start = ((s8[16777216]{0:T(1024)(128)(4,1)}), s8[4194304]{0:T(1024)(128)(4,1)S(1)}, s32[]{:S(2)}) async-start(s8[16777216]{0:T(1024)(128)(4,1)} %bitcast.94), calls=%async_computation.6 | async-start | bytes 8388608
  450.7 21.4 %slice-start.1 = ((s8[16777216]{0:T(1024)(128)(4,1)}), s8[4194304]{0:T(1024)(128)(4,1)S(1)}, s32[]{:S(2)}) async-start(s8[16777216]{0:T(1024)(128)(4,1)} %bitcast.94), calls=%async_computation.7 | async-start | bytes 8388608
  450.7 21.4 %slice-start.2 = ((s8[16777216]{0:T(1024)(128)(4,1)}), s8[4194304]{0:T(1024)(128)(4,1)S(1)}, s32[]{:S(2)}) async-start(s8[16777216]{0:T(1024)(128)(4,1)} %bitcast.94), calls=%async_computation.8 | async-start | bytes 8388608
  468.0 2.2 copy-start.1
  468.0 2.2 copy-start.2
  470.2 2.6 slice-start.3
  500.4 4.0 copy-start.6
  507.6 3.6 copy-start.4
  507.6 4.9 copy-start
  522.8 2.6 copy-start.12
  525.4 0.7 copy-start.10
  (2 other events, 1.3 us)
Sparse Core Ops, SparseCore 0:
  10.2 79.3 all-gather.2
  91.1 290.7 all-gather.4
  571.0 106.0 reduce-scatter.1
where the time goes:
time: 693 us; the launch traced here: 686 us
  waiting for transfers between devices  414 us (60%)
  local copies, waits for them, and re-layouts  119 us (17%)
  matrix products  96.2 us (14%)
  blocking collectives  21.1 us (3%)
  other arithmetic  16.3 us (2%)
  between operations  14.4 us (2%)
    all_gather x1, waiting for transfers between devices, shards(): weights = lax.all_gather(w_in, 'tp', axis=0, tiled=True)  290 us
    reduce_scatter x1, waiting for transfers between devices, shards(): lax.psum_scatter(lax.dot_general(weights, grad_rows, (((1,), (1,)), ((),...  106 us
    gather x2, local copies, waits for them, and re-layouts, long_filter(): current = jnp.where(distance >= 0, head_taps[:, clipped], 0.0)  80.2 us
    dot_general x2, matrix products, long_filter(): inside = jnp.einsum('cts,cbs->cbt', current, tiled, precision=HIGH)  44.9 us
    all_to_all x1, blocking collectives, shards(): lax.all_to_all(grad_rounded, 'tp', split_axis=0, concat_axis=1, tiled=True)  21.1 us
    dot_general x1, matrix products, shards(): projected = jnp.dot(features, weights, preferred_element_type=jnp.float32)  19.3 us
    dot_general x1, matrix products, shards(): lax.dot_general(weights, grad_rows, (((1,), (1,)), ((), ())), preferred_e...  19.1 us
    all_to_all x1, waiting for transfers between devices, shards(): lax.all_to_all(rounded, 'tp', split_axis=1, concat_axis=0, tiled=True)  15.8 us
  transfers between devices with their start and end apart: 4, of which 3 were waited for; matrix products, arithmetic and copies ran while one was open for 12% of the time, Pallas kernels for 0%

commit v1 on v0

--- a/solution.py
+++ b/solution.py
@@ -1,11 +1,15 @@
+import functools
 import math
 
 import jax
 import jax.numpy as jnp
 from jax import lax
+from jax.experimental import pallas as pl
+from jax.experimental.pallas import tpu as pltpu
 from jax.sharding import PartitionSpec as P
 
 HIGH = lax.Precision.HIGHEST
+LANES = 128
 
 
 def causal_taps(signal, taps):
@@ -80,7 +84,209 @@
     return (mixed_out.astype(jnp.bfloat16), summed)
 
 
+def swap_pairs(n_ctx, n_tp):
+    half = n_ctx // n_tp
+    pairs = []
+    for ctx in range(n_ctx):
+        for tp in range(n_tp):
+            owner = (tp * half + ctx % half) * n_tp + ctx // half
+            pairs.append((owner, ctx * n_tp + tp))
+    return pairs
+
+
+def mix_kernel(seq_len, chans, modes, chunks, proj_ref, spread_ref, taps_ref, rate_ref, res_ref,
+               cot_ref, mixed_ref, grad_ref, planes, feats, sums, grads, outs, backs, rates, powers):
+    halves = chans // LANES
+    rows = chunks * halves
+    steps = seq_len // chunks
+    tile = steps
+
+    def multiply(i, carry):
+        at = pl.ds(pl.multiple_of(i * tile, tile), tile)
+        planes[at, :] = jnp.dot(proj_ref[at, :], spread_ref[...], preferred_element_type=jnp.float32)
+        return carry
+
+    lax.fori_loop(0, chunks, multiply, 0)
+
+    row_id = lax.broadcasted_iota(jnp.int32, (seq_len, LANES), 0)
+    taps_count = taps_ref.shape[0]
+    for col in range(3 * halves):
+        lanes = slice(col * LANES, (col + 1) * LANES)
+        plane = planes[:, lanes]
+        total = plane * taps_ref[0:1, lanes]
+        for delay in range(1, taps_count):
+            shifted = jnp.where(row_id >= delay, pltpu.roll(plane, delay, 0), 0.0)
+            total = total + shifted * taps_ref[delay:delay + 1, lanes]
+        feats[:, lanes] = total
+
+    for half in range(halves):
+        lanes = [slice((r * halves + half) * LANES, (r * halves + half + 1) * LANES) for r in range(3)]
+        for chunk in range(chunks):
+            at = slice(chunk * steps, (chunk + 1) * steps)
+            row = pl.ds(chunk * halves + half, steps, stride=rows)
+            sums[row, :] = feats[at, lanes[1]] * feats[at, lanes[2]]
+            cot = cot_ref[half * LANES:(half + 1) * LANES, at].astype(jnp.float32).T
+            planes[at, half * LANES:(half + 1) * LANES] = cot
+            grads[row, :] = cot * feats[at, lanes[0]]
+
+    chunk_id = lax.broadcasted_iota(jnp.int32, (rows, LANES), 0) // halves
+    for m in range(modes):
+        rates[m] = jnp.exp(-rate_ref[m])
+        powers[m] = jnp.exp(-rate_ref[m] * float(steps))
+
+    def scan(source, result, backward):
+        def place(step):
+            at = steps - 1 - step if backward else step
+            return pl.ds(pl.multiple_of(at * rows, rows), rows)
+
+        def ends(step, states):
+            u = source[place(step), :]
+            return tuple(rates[m] * states[m] + u for m in range(modes))
+
+        zeros = tuple(jnp.zeros((rows, LANES), jnp.float32) for _ in range(modes))
+        last = lax.fori_loop(0, steps, ends, zeros, unroll=4)
+        first = []
+        for m in range(modes):
+            carry = jnp.zeros((rows, LANES), jnp.float32)
+            for _ in range(chunks - 1):
+                total = powers[m] * carry + last[m]
+                if backward:
+                    carry = jnp.where(chunk_id < chunks - 1, pltpu.roll(total, rows - halves, 0), 0.0)
+                else:
+                    carry = jnp.where(chunk_id > 0, pltpu.roll(total, halves, 0), 0.0)
+            first.append(carry)
+
+        def run(step, states):
+            u = source[place(step), :]
+            states = tuple(rates[m] * states[m] + u for m in range(modes))
+            terms = [res_ref[m] * states[m] for m in range(modes)]
+            while len(terms) > 1:
+                terms = [a + b for a, b in zip(terms[0::2], terms[1::2])]
+            result[place(step), :] = terms[0]
+            return states
+
+        lax.fori_loop(0, steps, run, tuple(first), unroll=4)
+
+    scan(sums, outs, False)
+    scan(grads, backs, True)
+
+    for half in range(halves):
+        lanes = [slice((r * halves + half) * LANES, (r * halves + half + 1) * LANES) for r in range(3)]
+        for chunk in range(chunks):
+            at = slice(chunk * steps, (chunk + 1) * steps)
+            row = pl.ds(chunk * halves + half, steps, stride=rows)
+            y = outs[row, :]
+            du = backs[row, :]
+            mixed_ref[half * LANES:(half + 1) * LANES, at] = (feats[at, lanes[0]] * y).T.astype(jnp.bfloat16)
+            cot = planes[at, half * LANES:(half + 1) * LANES]
+            key = feats[at, lanes[1]]
+            feats[at, lanes[0]] = cot * y
+            feats[at, lanes[1]] = du * feats[at, lanes[2]]
+            feats[at, lanes[2]] = du * key
+
+    for col in range(3 * halves):
+        lanes = slice(col * LANES, (col + 1) * LANES)
+        grad = feats[:, lanes]
+        total = grad * taps_ref[0:1, lanes]
+        for delay in range(1, taps_count):
+            shifted = jnp.where(row_id < seq_len - delay, pltpu.roll(grad, seq_len - delay, 0), 0.0)
+            total = total + shifted * taps_ref[delay:delay + 1, lanes]
+        planes[:, lanes] = total
+
+    def gather(i, carry):
+        at = pl.ds(pl.multiple_of(i * tile, tile), tile)
+        grad_ref[at, :] = lax.dot_general(
+            planes[at, :].astype(jnp.bfloat16), spread_ref[...], (((1,), (1,)), ((), ())),
+            preferred_element_type=jnp.float32,
+        ).astype(jnp.bfloat16)
+        return carry
+
+    lax.fori_loop(0, chunks, gather, 0)
+
+
+def mix(projected, short_taps, li_residue, li_rate, cotangent):
+    seq_len, cols = projected.shape
+    chans, modes = li_rate.shape
+    halves = chans // LANES
+    rows = 8
+    chunks = rows // halves
+    source = jnp.arange(cols)[:, None]
+    target = jnp.arange(cols)[None, :]
+    spread = (source == 3 * (target % chans) + target // chans).astype(jnp.bfloat16)
+    taps = short_taps.reshape(-1, chans, 3).transpose(0, 2, 1).reshape(-1, cols)
+
+    def per_row(values):
+        return jnp.tile(values.T.reshape(modes, halves, LANES), (1, chunks, 1))
+
+    f32 = functools.partial(pltpu.VMEM, dtype=jnp.float32)
+    vmem = pl.BlockSpec(memory_space=pltpu.VMEM)
+    return pl.pallas_call(
+        functools.partial(mix_kernel, seq_len, chans, modes, chunks),
+        out_shape=(
+            jax.ShapeDtypeStruct((chans, seq_len), jnp.bfloat16),
+            jax.ShapeDtypeStruct((seq_len, cols), jnp.bfloat16),
+        ),
+        in_specs=[vmem] * 6,
+        out_specs=(vmem, vmem),
+        scratch_shapes=[
+            f32((seq_len, cols)),
+            f32((seq_len, cols)),
+            f32((seq_len * halves, LANES)),
+            f32((seq_len * halves, LANES)),
+            f32((seq_len * halves, LANES)),
+            f32((seq_len * halves, LANES)),
+            f32((modes, rows, LANES)),
+            f32((modes, rows, LANES)),
+        ],
+        compiler_params=pltpu.CompilerParams(vmem_limit_bytes=40 * 1024 * 1024),
+        cost_estimate=pl.CostEstimate(
+            flops=20 * 10**9, bytes_accessed=6 * seq_len * cols, transcendentals=0
+        ),
+        name="mix",
+    )(projected, spread, taps, per_row(li_rate), per_row(li_residue), cotangent)
+
+
+def fast_shards(n_ctx, n_tp, tokens, w_in, short_taps, li_residue, li_rate, cotangent):
+    pairs = swap_pairs(n_ctx, n_tp)
+    tp = lax.axis_index("tp")
+    rows, cols = w_in.shape
+    half_cols = cols // 2
+    piece = lax.ppermute(tokens, ("ctx", "tp"), pairs)
+    features = lax.all_gather(piece, "ctx", axis=1, tiled=True)
+
+    def partial(side):
+        weights = lax.dynamic_slice_in_dim(w_in, side * half_cols, half_cols, 1)
+        return jnp.concatenate(
+            [
+                jnp.dot(features[:, i * rows:(i + 1) * rows], weights, preferred_element_type=jnp.float32)
+                for i in range(n_tp)
+            ],
+            axis=0,
+        )
+
+    other = lax.ppermute(partial(1 - tp).astype(jnp.bfloat16), "tp", [(0, 1), (1, 0)])
+    projected = (partial(tp) + other.astype(jnp.float32)).astype(jnp.bfloat16)
+    mixed, grad = mix(projected, short_taps, li_residue, li_rate, cotangent)
+    grad_cols = lax.all_gather(grad, "tp", axis=1, tiled=True)
+    count = tokens.shape[0]
+    products = jnp.concatenate(
+        [
+            lax.dot_general(
+                w_in, grad_cols[i * count:(i + 1) * count], (((1,), (1,)), ((), ())),
+                preferred_element_type=jnp.float32,
+            ).astype(jnp.bfloat16)
+            for i in range(n_tp)
+        ],
+        axis=0,
+    )
+    summed = lax.psum_scatter(products, "ctx", scatter_dimension=0, tiled=True)
+    back = [(b, a) for a, b in pairs]
+    return mixed, lax.ppermute(summed, ("ctx", "tp"), back)
+
+
 def solution(mesh):
+    n_ctx, n_tp = mesh.shape["ctx"], mesh.shape["tp"]
+    body = functools.partial(fast_shards, n_ctx, n_tp) if (n_ctx, n_tp) == (16, 2) else shards
     in_specs = (
         P("tp", "ctx"),
         P("tp", "ctx"),
@@ -90,4 +296,4 @@
         P(("ctx", "tp"), None),
     )
     out_specs = (P(("ctx", "tp"), None), P("ctx", "tp"))
-    return jax.shard_map(shards, mesh=mesh, in_specs=in_specs, out_specs=out_specs, check_vma=False)
+    return jax.shard_map(body, mesh=mesh, in_specs=in_specs, out_specs=out_specs, check_vma=False)

time: 693 us -> 402 us (0.58)
  waiting for transfers between devices: 414 us -> 297 us
  local copies, waits for them, and re-layouts: 119 us -> 2.33 us
  matrix products: 96.2 us -> 51.9 us
  blocking collectives: 21.1 us -> 0 us
  Pallas kernels: 0 us -> 16.9 us
    all_gather x2, waiting for transfers between devices: 290 us -> 120 us  [the longest x1 78.4 us: fast_shards(): features = lax.all_gather(piece, 'ctx', axis=1, tiled=True)]
    gather x2 -> x0, local copies, waits for them, and re-layouts: 80.2 us -> none  [long_filter(): current = jnp.where(distance >= 0, head_taps[:, clipped], 0.0)]
    ppermute x0 -> x3, waiting for transfers between devices: none -> 70.1 us  [the longest x1 24.8 us: fast_shards(): return (mixed, lax.ppermute(summed, ('ctx', 'tp'), back))]
    dot_general x8 -> x6, matrix products: 96.2 us -> 51.9 us  [the longest x4 27.5 us: partial(): jnp.dot(features[:, i * rows:(i + 1) * rows], weights, preferred_element_...]
    all_to_all x1 -> x0, blocking collectives: 21.1 us -> none  [shards(): lax.all_to_all(grad_rounded, 'tp', split_axis=0, concat_axis=1, tiled=True)]
    pallas_call x0 -> x1, Pallas kernels: none -> 16.9 us  [mix(): pl.pallas_call(functools.partial(mix_kernel, seq_len, chans, modes, chunk...]
    all_to_all x1 -> x0, waiting for transfers between devices: 15.8 us -> none  [shards(): lax.all_to_all(rounded, 'tp', split_axis=1, concat_axis=0, tiled=True)]
    reshape x3 -> x1, local copies, waits for them, and re-layouts: 11.5 us -> 0.28 us  [mix(): taps = short_taps.reshape(-1, chans, 3).transpose(0, 2, 1).reshape(-1, cols)]
  transfers between devices with their start and end apart: 4 -> 6, of which waited for: 3 -> 6; matrix products, arithmetic and copies ran while one was open for 12% -> 4% of each run, Pallas kernels for 0% -> 0%
where the time goes in v1:
time: 402 us; the launch traced here: 401 us
  waiting for transfers between devices  297 us (74%)
  matrix products  51.9 us (13%)
  Pallas kernels  16.9 us (4%)
  between operations  13.9 us (3%)
  other arithmetic  10.1 us (3%)
  starting transfers between devices  9.29 us (2%)
    reduce_scatter x1, waiting for transfers between devices, fast_shards(): summed = lax.psum_scatter(products, 'ctx', scatter_dimension=0, tiled=True)  106 us
    all_gather x1, waiting for transfers between devices, fast_shards(): features = lax.all_gather(piece, 'ctx', axis=1, tiled=True)  78.4 us
    all_gather x1, waiting for transfers between devices, fast_shards(): grad_cols = lax.all_gather(grad, 'tp', axis=1, tiled=True)  42.1 us
    dot_general x4, matrix products, partial(): jnp.dot(features[:, i * rows:(i + 1) * rows], weights, preferred_element_...  27.5 us
    ppermute x1, waiting for transfers between devices, fast_shards(): return (mixed, lax.ppermute(summed, ('ctx', 'tp'), back))  24.8 us
    dot_general x2, matrix products, fast_shards(): lax.dot_general(w_in, grad_cols[i * count:(i + 1) * count], (((1,), (1,))...  24.4 us
    ppermute x1, waiting for transfers between devices, fast_shards(): piece = lax.ppermute(tokens, ('ctx', 'tp'), pairs)  24.3 us
    ppermute x1, waiting for transfers between devices, fast_shards(): lax.ppermute(partial(1 - tp).astype(jnp.bfloat16), 'tp', [(0, 1), (1, 0)])  21 us
  transfers between devices with their start and end apart: 6, of which 6 were waited for; matrix products, arithmetic and copies ran while one was open for 4% of the time, Pallas kernels for 0%

profile of v1, /device:TPU:2, one launch (start us, length us, event | category | flops | bytes accessed | tf_op | source)
XLA Modules:
  0.0 401.3 jit_solution(2411635043846850832)
XLA Ops:
  7.2 4.5 %collective-permute-start = (bf16[512,512]{1,0:T(8,128)(2,1)}, bf16[512,512]{1,0:T(8,128)(2,1)S(1)}, u32[]{:S(2)}, u32[]{:S(2)}) collective-permute-start(bf16[512,512]{1,0:T(8,128)(2,1)} %param.6), channel_id=1, source_target_pairs={{0,0},{16,1},{2,2},{18,3},{4,4},{20,5},{6,6},{22,7},{8,8},{24,9},{... | collective-permute-start | bytes 1572872 | tf_op jit(solution)/shard_map/ppermute | solution.py:254
  11.7 24.3 %collective-permute-done = bf16[512,512]{1,0:T(8,128)(2,1)S(1)} collective-permute-done((bf16[512,512]{1,0:T(8,128)(2,1)}, bf16[512,512]{1,0:T(8,128)(2,1)S(1)}, u32[]{:S(2)}, u32[]{:S(2)}) %collective-permute-start) | collective-permute-done | bytes 524320 | tf_op jit(solution)/shard_map/ppermute | solution.py:254
  36.0 0.8 copy-done.1
  36.9 78.4 %all-gather.3.cloned.1.call-done = bf16[512,8192]{1,0:T(8,128)(2,1)} async-done(((bf16[512,512]{1,0:T(8,128)(2,1)}), bf16[512,8192]{1,0:T(8,128)(2,1)}) %all-gather.3.cloned.1.call-update) | async-done | bytes 8388624 | tf_op jit(solution)/shard_map/all_gather | solution.py:255
  115.3 7.6 %fusion.43 = bf16[512,768]{1,0:T(8,128)(2,1)S(1)} fusion(bf16[4096,1536]{1,0:T(8,128)(2,1)} %param.7, s32[]{:T(128)S(6)} %select_n.29, bf16[512,8192]{1,0:T(8,128)(2,1)} %all-gather.3.cloned.1.call-done), kind=kOutput, calls=%fused_computation.29 | convolution fusion | flops 3221618688 | bytes 11272196 | tf_op jit(solution)/shard_map/dot_general | solution.py:261
  122.9 5.8 %fusion.38 = bf16[512,768]{1,0:T(8,128)(2,1)S(1)} fusion(bf16[4096,1536]{1,0:T(8,128)(2,1)} %param.7, s32[]{:T(128)S(6)} %select_n.29, bf16[512,8192]{1,0:T(8,128)(2,1)S(1)} %copy-done.5), kind=kOutput, calls=%fused_computation.28 | convolution fusion | flops 3221618688 | bytes 11272196 | tf_op jit(solution)/shard_map/dot_general | solution.py:261
  128.8 0.1 pad_maximum_fusion.1
  128.9 0.6 collective-permute-start.1
  129.5 0.4 fusion.15.spread_ref
  130.0 0.3 reshape.73
  130.3 0.1 copy.10
  130.4 7.1 %fusion.23 = f32[512,768]{1,0:T(8,128)S(1)} fusion(bf16[4096,1536]{1,0:T(8,128)(2,1)} %param.7, s32[]{:T(128)S(6)} %select_n.28, bf16[512,8192]{1,0:T(8,128)(2,1)} %all-gather.3.cloned.1.call-done), kind=kOutput, calls=%fused_computation.25 | convolution fusion | flops 3221225472 | bytes 12058628 | tf_op jit(solution)/shard_map/dot_general | solution.py:261
  137.5 7.1 %fusion.18 = f32[512,768]{1,0:T(8,128)S(1)} fusion(bf16[4096,1536]{1,0:T(8,128)(2,1)} %param.7, s32[]{:T(128)S(6)} %select_n.28, bf16[512,8192]{1,0:T(8,128)(2,1)} %all-gather.3.cloned.1.call-done), kind=kOutput, calls=%fused_computation.24 | convolution fusion | flops 3221225472 | bytes 12058628 | tf_op jit(solution)/shard_map/dot_general | solution.py:261
  144.6 21.0 %collective-permute-done.1 = bf16[1024,768]{1,0:T(8,128)(2,1)} collective-permute-done((bf16[1024,768]{1,0:T(8,128)(2,1)S(1)}, bf16[1024,768]{1,0:T(8,128)(2,1)}, u32[]{:S(2)}, u32[]{:S(2)}) %collective-permute-start.1) | collective-permute-done | bytes 1572896 | tf_op jit(solution)/shard_map/ppermute | solution.py:267
  165.6 1.9 fusion.14.proj_ref
  167.5 16.9 %mix.1 = (bf16[256,1024]{1,0:T(8,128)(2,1)}, bf16[1024,768]{1,0:T(8,128)(2,1)}) custom-call(bf16[1024,768]{1,0:T(8,128)(2,1)S(1)} %fusion.14.proj_ref, bf16[768,768]{1,0:T(8,128)(2,1)S(1)} %fusion.15.spread_ref, f32[3,768]{1,0:T(4,128)S(1)} %bitcast.23, f32[16,8,128]{2,1,0:T(8,128)S(1)} %bitcast.21, f32[16,8,128]{2,1,0:T(8,128)S(1)} %bitcast.22, ...), custom_call_target="tpu_custom_call" | custom-call | flops 20000000000 | bytes 4718592 | tf_op jit(solution)/shard_map/mix/pallas_call | solution.py:223
  184.6 42.1 %all-gather.5.cloned.1.call-done = bf16[1024,1536]{1,0:T(8,128)(2,1)} async-done(((bf16[1024,768]{1,0:T(8,128)(2,1)}), bf16[1024,1536]{1,0:T(8,128)(2,1)}) %all-gather.5.cloned.1.call-update) | async-done | bytes 3145744 | tf_op jit(solution)/shard_map/all_gather | solution.py:270
  226.6 11.6 %fusion.9 = bf16[4096,512]{0,1:T(8,128)(2,1)} fusion(bf16[4096,1536]{1,0:T(8,128)(2,1)} %param.7, bf16[1024,1536]{1,0:T(8,128)(2,1)} %all-gather.5.cloned.1.call-done), kind=kOutput, calls=%fused_computation.12 | convolution fusion | flops 6444548096 | bytes 18350080 | tf_op jit(solution)/shard_map/dot_general | solution.py:274
  238.2 12.8 %fusion.8 = bf16[4096,512]{0,1:T(8,128)(2,1)} fusion(bf16[4096,1536]{1,0:T(8,128)(2,1)} %param.7, bf16[1024,1536]{1,0:T(8,128)(2,1)S(1)} %copy-done.6), kind=kOutput, calls=%fused_computation.11 | convolution fusion | flops 6444548096 | bytes 18350080 | tf_op jit(solution)/shard_map/dot_general | solution.py:274
  251.0 7.7 %pad_maximum_fusion = bf16[8192,512]{0,1:T(8,128)(2,1)} fusion(bf16[4096,512]{0,1:T(8,128)(2,1)} %fusion.9, bf16[4096,512]{0,1:T(8,128)(2,1)} %fusion.8), kind=kLoop, calls=%fused_computation | loop fusion | flops 16777216 | bytes 16777216 | tf_op jit(solution)/shard_map/concatenate | solution.py:272
  258.7 106.2 %reduce-scatter.2.cloned.1.call-done = bf16[512,512]{0,1:T(8,128)(2,1)} async-done(((bf16[8192,512]{0,1:T(8,128)(2,1)}), bf16[512,512]{0,1:T(8,128)(2,1)}) %reduce-scatter.2.cloned.1.call-update) | async-done | bytes 524304 | tf_op jit(solution)/shard_map/reduce_scatter | solution.py:282
  364.9 4.1 %collective-permute-start.2 = (bf16[512,512]{0,1:T(8,128)(2,1)}, bf16[512,512]{0,1:T(8,128)(2,1)S(1)}, u32[]{:S(2)}, u32[]{:S(2)}) collective-permute-start(bf16[512,512]{0,1:T(8,128)(2,1)} %reduce-scatter.2.cloned.1.call-done), channel_id=1, source_target_pairs={{0,0},{1,16},{2,2},{3,18},{4,4},{5,20},{6,6},{7,22},{8,8},{9,24},{... | collective-permute-start | bytes 1572872 | tf_op jit(solution)/shard_map/ppermute | solution.py:284
  369.0 24.8 %collective-permute-done.2 = bf16[512,512]{0,1:T(8,128)(2,1)S(1)} collective-permute-done((bf16[512,512]{0,1:T(8,128)(2,1)}, bf16[512,512]{0,1:T(8,128)(2,1)S(1)}, u32[]{:S(2)}, u32[]{:S(2)}) %collective-permute-start.2) | collective-permute-done | bytes 524320 | tf_op jit(solution)/shard_map/ppermute | solution.py:284
  393.7 1.0 copy.11
  (25 shorter events, 0.3 us)
Async XLA Ops:
  7.2 108.1 %all-gather.3.cloned.1.call-start = ((), (), s32[]{:S(2)}) async-start(), calls=%async_computation.1 | async-start | bytes 8912896 | tf_op jit(solution)/shard_map/all_gather | solution.py:255
  7.2 28.8 %collective-permute-start = (bf16[512,512]{1,0:T(8,128)(2,1)}, bf16[512,512]{1,0:T(8,128)(2,1)S(1)}, u32[]{:S(2)}, u32[]{:S(2)}) collective-permute-start(bf16[512,512]{1,0:T(8,128)(2,1)} %param.6), channel_id=1, source_target_pairs={{0,0},{16,1},{2,2},{18,3},{4,4},{20,5},{6,6},{22,7},{8,8},{24,9},{... | collective-permute-start | bytes 1572872 | tf_op jit(solution)/shard_map/ppermute | solution.py:254
  36.0 0.8 copy-start.1
  36.8 189.8 %all-gather.5.cloned.1.call-start = ((), (), s32[]{:S(2)}) async-start(), calls=%async_computation.2 | async-start | bytes 4718592 | tf_op jit(solution)/shard_map/all_gather | solution.py:270
  115.3 7.6 %copy-start.5 = (bf16[512,8192]{1,0:T(8,128)(2,1)S(1)}, bf16[512,8192]{1,0:T(8,128)(2,1)}, u32[]{:S(2)}) copy-start(bf16[512,8192]{1,0:T(8,128)(2,1)} %all-gather.3.cloned.1.call-done) | copy-start | bytes 25165828
  128.7 1.2 copy-start.2
  128.7 1.2 copy-start.3
  128.7 1.2 copy-start.4
  128.9 36.7 %collective-permute-start.1 = (bf16[1024,768]{1,0:T(8,128)(2,1)S(1)}, bf16[1024,768]{1,0:T(8,128)(2,1)}, u32[]{:S(2)}, u32[]{:S(2)}) collective-permute-start(bf16[1024,768]{1,0:T(8,128)(2,1)S(1)} %pad_maximum_fusion.1), channel_id=1, source_target_pairs={{0,1},{1,0},{2,3},{3,2},{4,5},{5,4},{6,7},{7,6},{8,9},{9,8},{10,11... | collective-permute-start | bytes 4718600 | tf_op jit(solution)/shard_map/ppermute | solution.py:267
  144.5 23.0 %copy-start = (bf16[256,1024]{1,0:T(8,128)(2,1)S(1)}, bf16[256,1024]{1,0:T(8,128)(2,1)}, u32[]{:S(2)}) copy-start(bf16[256,1024]{1,0:T(8,128)(2,1)} %cot_ref.1) | copy-start | bytes 1572868
  184.5 180.4 %reduce-scatter.2.cloned.1.call-start = ((), (), s32[]{:S(2)}) async-start(), calls=%async_computation.3 | async-start | bytes 8912896 | tf_op jit(solution)/shard_map/reduce_scatter | solution.py:282
  226.6 11.6 %copy-start.6 = (bf16[1024,1536]{1,0:T(8,128)(2,1)S(1)}, bf16[1024,1536]{1,0:T(8,128)(2,1)}, u32[]{:S(2)}) copy-start(bf16[1024,1536]{1,0:T(8,128)(2,1)} %all-gather.5.cloned.1.call-done) | copy-start | bytes 9437188
  364.9 28.8 %collective-permute-start.2 = (bf16[512,512]{0,1:T(8,128)(2,1)}, bf16[512,512]{0,1:T(8,128)(2,1)S(1)}, u32[]{:S(2)}, u32[]{:S(2)}) collective-permute-start(bf16[512,512]{0,1:T(8,128)(2,1)} %reduce-scatter.2.cloned.1.call-done), channel_id=1, source_target_pairs={{0,0},{1,16},{2,2},{3,18},{4,4},{5,20},{6,6},{7,22},{8,8},{9,24},{... | collective-permute-start | bytes 1572872 | tf_op jit(solution)/shard_map/ppermute | solution.py:284
Sparse Core Ops, SparseCore 0:
  36.9 78.2 all-gather.2
  184.6 41.9 all-gather.4
  258.8 105.9 reduce-scatter.1

commit v2 on v1

--- a/solution.py
+++ b/solution.py
@@ -82,6 +82,187 @@
         tiled=True,
     )
     return (mixed_out.astype(jnp.bfloat16), summed)
+
+
+MESH = pl.DeviceIdType.MESH
+TURNS = (4, 3, -3, 2, -2, 1, -1, 0)
+
+
+def ring_place(ctx):
+    z, y = ctx // 4, (ctx // 2) % 2
+    return z + y * (7 - 2 * z)
+
+
+def ring_ctx(place, core):
+    y = place // 4
+    z = place + y * (7 - 2 * place)
+    return z * 4 + y * 2 + core
+
+
+def greet(others, partner, ctx, tp):
+    barrier = pltpu.get_barrier_semaphore()
+    for other in others:
+        pl.semaphore_signal(barrier, inc=1, device_id=other, device_id_type=MESH)
+
+    @pl.when(ctx // 8 != tp)
+    def _():
+        pl.semaphore_signal(barrier, inc=1, device_id=partner, device_id_type=MESH)
+        pl.semaphore_wait(barrier, len(others) + 1)
+
+    @pl.when(ctx // 8 == tp)
+    def _():
+        pl.semaphore_wait(barrier, len(others))
+
+
+def scatter_kernel(grad_ref, w_hbm, out_ref, w_ref, cols, own, core_send, core_recv, right_send, right_recv,
+                   left_send, left_recv, last, landed, local_sem, x_ssem, x_rsem, core_ssem, core_rsem,
+                   r_ssem, r_rsem, l_ssem, l_rsem, end_ssem, end_rsem):
+    ctx, tp = lax.axis_index("ctx"), lax.axis_index("tp")
+    core, place = ctx % 2, ring_place(ctx)
+    across = (ctx, 1 - tp)
+    beside = (ctx + 1 - 2 * core, tp)
+    right = (ring_ctx((place + 1) % 8, core), tp)
+    left = (ring_ctx((place + 7) % 8, core), tp)
+    owner = (tp * 8 + ctx % 8, ctx // 8)
+    count, width = own.shape[2], grad_ref.shape[1]
+    load = pltpu.make_async_copy(w_hbm, w_ref, local_sem.at[0])
+    load.start()
+    keep = pltpu.make_async_copy(grad_ref, cols.at[tp], local_sem.at[1])
+    keep.start()
+    greet([across, beside, right, left], owner, ctx, tp)
+
+    def send(src, dst, ssem, rsem, where):
+        copy = pltpu.make_async_remote_copy(
+            src_ref=src, dst_ref=dst, send_sem=ssem, recv_sem=rsem, device_id=where, device_id_type=MESH
+        )
+        copy.start()
+        return copy
+
+    near = ctx // 8
+    shares = []
+    for turn, half in enumerate((1 - near, near)):
+        at = pl.ds(pl.multiple_of(half * count, count), count)
+        shares.append(send(grad_ref.at[at], cols.at[tp, at], x_ssem.at[turn], x_rsem.at[turn], across))
+    load.wait()
+    keep.wait()
+
+    def product(piece, dst):
+        row = (piece % 8) * count
+        token = pl.ds(pl.multiple_of((piece // 8) * count, count), count)
+
+        def tile(i, carry):
+            at = pl.ds(pl.multiple_of(row + i * 256, 256), 256)
+            total = None
+            for side in range(2):
+                term = lax.dot_general(
+                    w_ref[at, side * width:(side + 1) * width], cols[side, token, :],
+                    (((1,), (1,)), ((), ())), preferred_element_type=jnp.float32,
+                )
+                total = term if total is None else total + term
+            dst[pl.ds(pl.multiple_of(i * 256, 256), 256), :] = total.astype(dst.dtype)
+            return carry
+
+        lax.fori_loop(0, count // 256, tile, 0)
+
+    to_core = [None] * 8
+
+    def both(k):
+        target = (place + TURNS[k] + 8) % 8
+        product(ring_ctx(target, 1 - core), core_send.at[k])
+        to_core[k] = send(core_send.at[k], core_recv.at[k], core_ssem.at[k], core_rsem.at[k], beside)
+        product(ring_ctx(target, core), own.at[k])
+
+    def mine(k, rows):
+        return own[k, rows, :] + core_recv[k, rows, :].astype(jnp.float32)
+
+    top, bottom, whole = slice(0, count // 2), slice(count // 2, count), slice(0, count)
+    shares[0].wait_recv()
+    both(0)
+    shares[1].wait_recv()
+    to_core[0].wait_recv()
+    right_send[0, top, :] = mine(0, top).astype(jnp.bfloat16)
+    left_send[0, bottom, :] = mine(0, bottom).astype(jnp.bfloat16)
+    to_right = [send(right_send.at[0, top], right_recv.at[0, top], r_ssem.at[0], r_rsem.at[0], right)]
+    to_left = [send(left_send.at[0, bottom], left_recv.at[0, bottom], l_ssem.at[0], l_rsem.at[0], left)]
+    for k in (1, 2, 3, 4):
+        both(k)
+    for step in (1, 2, 3):
+        k = 2 * step - 1
+        to_core[k].wait_recv()
+        to_right[step - 1].wait_recv()
+        if step == 1:
+            right_send[1, top, :] = (mine(k, top) + right_recv[0, top, :].astype(jnp.float32)).astype(jnp.bfloat16)
+            right_send[1, bottom, :] = mine(k, bottom).astype(jnp.bfloat16)
+        else:
+            right_send[step] = (mine(k, whole) + right_recv[step - 1].astype(jnp.float32)).astype(jnp.bfloat16)
+        to_right.append(send(right_send.at[step], right_recv.at[step], r_ssem.at[step], r_rsem.at[step], right))
+        k += 1
+        to_core[k].wait_recv()
+        to_left[step - 1].wait_recv()
+        if step == 1:
+            left_send[1, top, :] = mine(k, top).astype(jnp.bfloat16)
+            left_send[1, bottom, :] = (mine(k, bottom) + left_recv[0, bottom, :].astype(jnp.float32)).astype(jnp.bfloat16)
+        else:
+            left_send[step] = (mine(k, whole) + left_recv[step - 1].astype(jnp.float32)).astype(jnp.bfloat16)
+        to_left.append(send(left_send.at[step], left_recv.at[step], l_ssem.at[step], l_rsem.at[step], left))
+        if step == 1:
+            for k in (5, 6, 7):
+                both(k)
+    to_core[7].wait_recv()
+    to_right[3].wait_recv()
+    to_left[3].wait_recv()
+    total = mine(7, whole) + right_recv[3].astype(jnp.float32) + left_recv[3].astype(jnp.float32)
+    last[...] = total.astype(jnp.bfloat16)
+
+    @pl.when(near != tp)
+    def _():
+        end = send(last, landed, end_ssem, end_rsem, owner)
+        end.wait()
+        out_ref[...] = landed[...]
+
+    @pl.when(near == tp)
+    def _():
+        out_ref[...] = last[...]
+
+    for copy in shares + to_core + to_right + to_left:
+        copy.wait_send()
+
+
+def multiply_scatter(w_in, grad):
+    rows, cols = w_in.shape
+    seq_len, width = grad.shape
+    block = rows // 8
+    bf16 = functools.partial(pltpu.VMEM, dtype=jnp.bfloat16)
+    dma = pltpu.SemaphoreType.DMA
+    vmem = pl.BlockSpec(memory_space=pltpu.VMEM)
+    return pl.pallas_call(
+        scatter_kernel,
+        out_shape=jax.ShapeDtypeStruct((block, block), jnp.bfloat16),
+        in_specs=[vmem, pl.BlockSpec(memory_space=pl.ANY)],
+        out_specs=vmem,
+        scratch_shapes=[
+            bf16((rows, cols)),
+            bf16((2, seq_len, width)),
+            pltpu.VMEM((8, block, block), jnp.float32),
+            bf16((8, block, block)),
+            bf16((8, block, block)),
+            bf16((4, block, block)),
+            bf16((4, block, block)),
+            bf16((4, block, block)),
+            bf16((4, block, block)),
+            bf16((block, block)),
+            bf16((block, block)),
+            dma((2,)), dma((2,)), dma((2,)), dma((8,)), dma((8,)),
+            dma((4,)), dma((4,)), dma((4,)), dma((4,)), dma, dma,
+        ],
+        compiler_params=pltpu.CompilerParams(
+            collective_id=1, has_side_effects=True, vmem_limit_bytes=56 * 1024 * 1024
+        ),
+        cost_estimate=pl.CostEstimate(
+            flops=2 * rows * cols * seq_len, bytes_accessed=2 * rows * cols, transcendentals=0
+        ),
+        name="multiply_scatter",
+    )(grad, w_in)
 
 
 def swap_pairs(n_ctx, n_tp):
@@ -267,21 +448,7 @@
     other = lax.ppermute(partial(1 - tp).astype(jnp.bfloat16), "tp", [(0, 1), (1, 0)])
     projected = (partial(tp) + other.astype(jnp.float32)).astype(jnp.bfloat16)
     mixed, grad = mix(projected, short_taps, li_residue, li_rate, cotangent)
-    grad_cols = lax.all_gather(grad, "tp", axis=1, tiled=True)
-    count = tokens.shape[0]
-    products = jnp.concatenate(
-        [
-            lax.dot_general(
-                w_in, grad_cols[i * count:(i + 1) * count], (((1,), (1,)), ((), ())),
-                preferred_element_type=jnp.float32,
-            ).astype(jnp.bfloat16)
-            for i in range(n_tp)
-        ],
-        axis=0,
-    )
-    summed = lax.psum_scatter(products, "ctx", scatter_dimension=0, tiled=True)
-    back = [(b, a) for a, b in pairs]
-    return mixed, lax.ppermute(summed, ("ctx", "tp"), back)
+    return mixed, multiply_scatter(w_in, grad)
 
 
 def solution(mesh):

time: 402 us -> 301 us (0.75)
  waiting for transfers between devices: 297 us -> 124 us
  Pallas kernels: 16.9 us -> 123 us
  matrix products: 51.9 us -> 27.6 us
  other arithmetic: 10.1 us -> 2.41 us
  starting transfers between devices: 9.29 us -> 5.13 us
    pallas_call x0 -> x1, Pallas kernels: none -> 107 us  [multiply_scatter(): pl.pallas_call(scatter_kernel, out_shape=jax.ShapeDtypeStruct((block, blo...]
    reduce_scatter x1 -> x0, waiting for transfers between devices: 106 us -> none  [fast_shards(): summed = lax.psum_scatter(products, 'ctx', scatter_dimension=0, tiled=True)]
    all_gather x1 -> x0, waiting for transfers between devices: 42.1 us -> none  [fast_shards(): grad_cols = lax.all_gather(grad, 'tp', axis=1, tiled=True)]
    ppermute x1 -> x0, waiting for transfers between devices: 24.8 us -> none  [fast_shards(): return (mixed, lax.ppermute(summed, ('ctx', 'tp'), back))]
    dot_general x2 -> x0, matrix products: 24.4 us -> none  [fast_shards(): lax.dot_general(w_in, grad_cols[i * count:(i + 1) * count], (((1,), (1,))...]
    concatenate x1 -> x0, other arithmetic: 7.69 us -> none  [fast_shards(): jnp.concatenate([lax.dot_general(w_in, grad_cols[i * count:(i + 1) * coun...]
    ppermute x1 -> x0, starting transfers between devices: 4.07 us -> none  [fast_shards(): return (mixed, lax.ppermute(summed, ('ctx', 'tp'), back))]
  transfers between devices with their start and end apart: 6 -> 3, of which waited for: 6 -> 3; matrix products, arithmetic and copies ran while one was open for 4% -> 5% of each run, Pallas kernels for 0% -> 0%
where the time goes in v2:
time: 301 us
  waiting for transfers between devices  124 us (41%)
  Pallas kernels  123 us (41%)
  matrix products  27.6 us (9%)
  between operations  14.2 us (5%)
  starting transfers between devices  5.13 us (2%)
  local copies, waits for them, and re-layouts  4.36 us (1%)
    pallas_call x1, Pallas kernels, multiply_scatter(): pl.pallas_call(scatter_kernel, out_shape=jax.ShapeDtypeStruct((block, blo...  107 us
    all_gather x1, waiting for transfers between devices, fast_shards(): features = lax.all_gather(piece, 'ctx', axis=1, tiled=True)  78.4 us
    dot_general x4, matrix products, partial(): jnp.dot(features[:, i * rows:(i + 1) * rows], weights, preferred_element_...  27.6 us
    ppermute x1, waiting for transfers between devices, fast_shards(): piece = lax.ppermute(tokens, ('ctx', 'tp'), pairs)  24.3 us
    ppermute x1, waiting for transfers between devices, fast_shards(): lax.ppermute(partial(1 - tp).astype(jnp.bfloat16), 'tp', [(0, 1), (1, 0)])  21 us
    pallas_call x1, Pallas kernels, mix(): pl.pallas_call(functools.partial(mix_kernel, seq_len, chans, modes, chunk...  16.1 us
  transfers between devices with their start and end apart: 3, of which 3 were waited for; matrix products, arithmetic and copies ran while one was open for 5% of the time, Pallas kernels for 0%

profile of v2, /device:TPU:2, one launch (start us, length us, event | category | flops | bytes accessed | tf_op | source)
XLA Modules:
  0.0 300.8 jit_solution(13715703333626089024)
XLA Ops:
  7.2 0.0 all-gather.2.cloned.1.call-start
  7.2 4.5 %collective-permute-start = (bf16[512,512]{1,0:T(8,128)(2,1)}, bf16[512,512]{1,0:T(8,128)(2,1)S(1)}, u32[]{:S(2)}, u32[]{:S(2)}) collective-permute-start(bf16[512,512]{1,0:T(8,128)(2,1)} %param.6), channel_id=1, source_target_pairs={{0,0},{16,1},{2,2},{18,3},{4,4},{20,5},{6,6},{22,7},{8,8},{24,9},{... | collective-permute-start | bytes 1572872 | tf_op jit(solution)/shard_map/ppermute | solution.py:435
  11.7 24.3 %collective-permute-done = bf16[512,512]{1,0:T(8,128)(2,1)S(1)} collective-permute-done((bf16[512,512]{1,0:T(8,128)(2,1)}, bf16[512,512]{1,0:T(8,128)(2,1)S(1)}, u32[]{:S(2)}, u32[]{:S(2)}) %collective-permute-start) | collective-permute-done | bytes 524320 | tf_op jit(solution)/shard_map/ppermute | solution.py:435
  36.0 0.8 copy-done.2
  36.8 0.0 all-gather.2.cloned.1.call-update
  36.8 78.4 %all-gather.2.cloned.1.call-done = bf16[512,8192]{1,0:T(8,128)(2,1)} async-done(((bf16[512,512]{1,0:T(8,128)(2,1)}), bf16[512,8192]{1,0:T(8,128)(2,1)}) %all-gather.2.cloned.1.call-update) | async-done | bytes 8388624 | tf_op jit(solution)/shard_map/all_gather | solution.py:436
  115.3 7.6 %fusion.34 = bf16[512,768]{1,0:T(8,128)(2,1)S(1)} fusion(bf16[4096,1536]{1,0:T(8,128)(2,1)} %w_hbm.1, s32[]{:T(128)S(6)} %select_n.29, bf16[512,8192]{1,0:T(8,128)(2,1)} %all-gather.2.cloned.1.call-done), kind=kOutput, calls=%fused_computation.21 | convolution fusion | flops 3221618688 | bytes 11272196 | tf_op jit(solution)/shard_map/dot_general | solution.py:442
  122.9 5.8 %fusion.39 = bf16[512,768]{1,0:T(8,128)(2,1)S(1)} fusion(bf16[4096,1536]{1,0:T(8,128)(2,1)} %w_hbm.1, s32[]{:T(128)S(6)} %select_n.29, bf16[512,8192]{1,0:T(8,128)(2,1)S(1)} %copy-done.6), kind=kOutput, calls=%fused_computation.22 | convolution fusion | flops 3221618688 | bytes 11272196 | tf_op jit(solution)/shard_map/dot_general | solution.py:442
  128.7 0.0 copy-start.5
  128.7 0.0 copy-start.3
  128.8 0.1 pad_maximum_fusion
  128.9 0.6 collective-permute-start.1
  129.5 0.4 fusion.13.spread_ref
  129.9 0.3 reshape.73
  130.2 0.1 copy.9
  130.4 7.1 %fusion.14 = f32[512,768]{1,0:T(8,128)S(1)} fusion(bf16[4096,1536]{1,0:T(8,128)(2,1)} %w_hbm.1, s32[]{:T(128)S(6)} %select_n.28, bf16[512,8192]{1,0:T(8,128)(2,1)} %all-gather.2.cloned.1.call-done), kind=kOutput, calls=%fused_computation.17 | convolution fusion | flops 3221225472 | bytes 12058628 | tf_op jit(solution)/shard_map/dot_general | solution.py:442
  137.5 7.1 %fusion.19 = f32[512,768]{1,0:T(8,128)S(1)} fusion(bf16[4096,1536]{1,0:T(8,128)(2,1)} %w_hbm.1, s32[]{:T(128)S(6)} %select_n.28, bf16[512,8192]{1,0:T(8,128)(2,1)} %all-gather.2.cloned.1.call-done), kind=kOutput, calls=%fused_computation.18 | convolution fusion | flops 3221225472 | bytes 12058628 | tf_op jit(solution)/shard_map/dot_general | solution.py:442
  144.6 0.0 copy-start
  144.6 21.0 %collective-permute-done.1 = bf16[1024,768]{1,0:T(8,128)(2,1)} collective-permute-done((bf16[1024,768]{1,0:T(8,128)(2,1)S(1)}, bf16[1024,768]{1,0:T(8,128)(2,1)}, u32[]{:S(2)}, u32[]{:S(2)}) %collective-permute-start.1) | collective-permute-done | bytes 1572896 | tf_op jit(solution)/shard_map/ppermute | solution.py:448
  165.6 1.9 fusion.12.proj_ref
  167.5 16.1 %mix.1 = (bf16[256,1024]{1,0:T(8,128)(2,1)}, bf16[1024,768]{1,0:T(8,128)(2,1)S(1)}) custom-call(bf16[1024,768]{1,0:T(8,128)(2,1)S(1)} %fusion.12.proj_ref, bf16[768,768]{1,0:T(8,128)(2,1)S(1)} %fusion.13.spread_ref, f32[3,768]{1,0:T(4,128)S(1)} %bitcast.17, f32[16,8,128]{2,1,0:T(8,128)S(1)} %bitcast.15, f32[16,8,128]{2,1,0:T(8,128)S(1)} %bitcast.16, ...), custom_call_target="tpu_custom_call" | custom-call | flops 20000000000 | bytes 4718592 | tf_op jit(solution)/shard_map/mix/pallas_call | solution.py:404
  183.6 1.2 copy-done.1
  184.8 107.3 %multiply_scatter.1 = bf16[512,512]{1,0:T(8,128)(2,1)} custom-call(bf16[1024,768]{1,0:T(8,128)(2,1)} %copy-done.1, bf16[4096,1536]{1,0:T(8,128)(2,1)} %w_hbm.1), custom_call_target="tpu_custom_call" | custom-call | flops 12884901888 | bytes 12582912 | tf_op jit(solution)/shard_map/multiply_scatter/pallas_call | solution.py:238
  292.1 1.9 copy.12
  (15 shorter events, 0.1 us)
Async XLA Ops:
  7.2 108.1 %all-gather.2.cloned.1.call-start = ((), (), s32[]{:S(2)}) async-start(), calls=%async_computation | async-start | bytes 8912896 | tf_op jit(solution)/shard_map/all_gather | solution.py:436
  7.2 28.8 %collective-permute-start = (bf16[512,512]{1,0:T(8,128)(2,1)}, bf16[512,512]{1,0:T(8,128)(2,1)S(1)}, u32[]{:S(2)}, u32[]{:S(2)}) collective-permute-start(bf16[512,512]{1,0:T(8,128)(2,1)} %param.6), channel_id=1, source_target_pairs={{0,0},{16,1},{2,2},{18,3},{4,4},{20,5},{6,6},{22,7},{8,8},{24,9},{... | collective-permute-start | bytes 1572872 | tf_op jit(solution)/shard_map/ppermute | solution.py:435
  36.0 0.8 copy-start.2
  115.3 7.6 %copy-start.6 = (bf16[512,8192]{1,0:T(8,128)(2,1)S(1)}, bf16[512,8192]{1,0:T(8,128)(2,1)}, u32[]{:S(2)}) copy-start(bf16[512,8192]{1,0:T(8,128)(2,1)} %all-gather.2.cloned.1.call-done) | copy-start | bytes 25165828
  128.7 1.2 copy-start.5
  128.7 1.6 copy-start.3
  128.7 1.6 copy-start.4
  128.9 36.7 %collective-permute-start.1 = (bf16[1024,768]{1,0:T(8,128)(2,1)S(1)}, bf16[1024,768]{1,0:T(8,128)(2,1)}, u32[]{:S(2)}, u32[]{:S(2)}) collective-permute-start(bf16[1024,768]{1,0:T(8,128)(2,1)S(1)} %pad_maximum_fusion), channel_id=1, source_target_pairs={{0,1},{1,0},{2,3},{3,2},{4,5},{5,4},{6,7},{7,6},{8,9},{9,8},{10,11... | collective-permute-start | bytes 4718600 | tf_op jit(solution)/shard_map/ppermute | solution.py:448
  144.6 22.9 %copy-start = (bf16[256,1024]{1,0:T(8,128)(2,1)S(1)}, bf16[256,1024]{1,0:T(8,128)(2,1)}, u32[]{:S(2)}) copy-start(bf16[256,1024]{1,0:T(8,128)(2,1)} %cot_ref.1) | copy-start | bytes 1572868
  183.6 1.2 copy-start.1
Sparse Core Ops, SparseCore 0:
  36.9 78.2 all-gather.1

commit v3 on v2

--- a/solution.py
+++ b/solution.py
@@ -265,14 +265,150 @@
     )(grad, w_in)
 
 
-def swap_pairs(n_ctx, n_tp):
-    half = n_ctx // n_tp
-    pairs = []
-    for ctx in range(n_ctx):
-        for tp in range(n_tp):
-            owner = (tp * half + ctx % half) * n_tp + ctx // half
-            pairs.append((owner, ctx * n_tp + tp))
-    return pairs
+def gather_kernel(tokens_ref, w_hbm, proj_ref, w_ref, pieces, total, part_send, part_recv, local_sem,
+                  swap_ssem, swap_rsem, core_ssem, core_rsem, r_ssem, r_rsem, l_ssem, l_rsem, x_ssem, x_rsem):
+    ctx, tp = lax.axis_index("ctx"), lax.axis_index("tp")
+    core, place = ctx % 2, ring_place(ctx)
+    across = (ctx, 1 - tp)
+    beside = (ctx + 1 - 2 * core, tp)
+    right = (ring_ctx((place + 1) % 8, core), tp)
+    left = (ring_ctx((place + 7) % 8, core), tp)
+    owner = (tp * 8 + ctx % 8, ctx // 8)
+    near = ctx // 8
+    count, width = tokens_ref.shape[0], proj_ref.shape[1]
+    load = pltpu.make_async_copy(w_hbm, w_ref, local_sem.at[0])
+    load.start()
+    greet([across, beside, right, left], owner, ctx, tp)
+
+    def send(src, dst, ssem, rsem, where):
+        copy = pltpu.make_async_remote_copy(
+            src_ref=src, dst_ref=dst, send_sem=ssem, recv_sem=rsem, device_id=where, device_id_type=MESH
+        )
+        copy.start()
+        return copy
+
+    def pass_on(place_of, ssem, rsem, where, rows=None):
+        piece = ring_ctx(place_of, core)
+        ref = pieces.at[piece] if rows is None else pieces.at[piece, rows]
+        return send(ref, ref, ssem, rsem, where)
+
+    def at_place(turn):
+        return (place + turn + 8) % 8
+
+    @pl.when(near != tp)
+    def _():
+        swap = send(tokens_ref, pieces.at[owner[0]], swap_ssem, swap_rsem, owner)
+        total[...] = jnp.zeros_like(total)
+        swap.wait()
+
+    @pl.when(near == tp)
+    def _():
+        keep = pltpu.make_async_copy(tokens_ref, pieces.at[ctx], local_sem.at[1])
+        keep.start()
+        keep.wait()
+
+    to_right = [pass_on(place, r_ssem.at[0], r_rsem.at[0], right)]
+    to_left = [pass_on(place, l_ssem.at[0], l_rsem.at[0], left)]
+    to_core = [pass_on(place, core_ssem.at[0], core_rsem.at[0], beside)]
+
+    @pl.when(near == tp)
+    def _():
+        total[...] = jnp.zeros_like(total)
+
+    load.wait()
+
+    def add(piece, side):
+        row = pl.ds(pl.multiple_of((piece % 8) * count, count), count)
+        lanes = pl.ds(pl.multiple_of(side * width, LANES), width)
+        token = (piece // 8) * count
+
+        def tile(i, carry):
+            at = pl.ds(pl.multiple_of(token + i * 256, 256), 256)
+            block = pieces[piece, pl.ds(pl.multiple_of(i * 256, 256), 256), :]
+            total[side, at, :] += jnp.dot(block, w_ref[row, lanes], preferred_element_type=jnp.float32)
+            return carry
+
+        lax.fori_loop(0, count // 256, tile, 0)
+
+    def add_place(turn, whose):
+        for side in range(2):
+            add(ring_ctx(at_place(turn), whose), side)
+
+    add_place(0, core)
+    top, bottom = slice(0, count // 2), slice(count // 2, count)
+    for step in (1, 2, 3):
+        to_right[step - 1].wait_recv()
+        to_right.append(pass_on(at_place(-step), r_ssem.at[step], r_rsem.at[step], right, top if step == 3 else None))
+        to_core.append(pass_on(at_place(-step), core_ssem.at[2 * step - 1], core_rsem.at[2 * step - 1], beside))
+        to_left[step - 1].wait_recv()
+        to_left.append(pass_on(at_place(step), l_ssem.at[step], l_rsem.at[step], left, bottom if step == 3 else None))
+        to_core.append(pass_on(at_place(step), core_ssem.at[2 * step], core_rsem.at[2 * step], beside))
+        add_place(-step, core)
+        add_place(step, core)
+        if step == 1:
+            to_core[0].wait_recv()
+            add_place(0, 1 - core)
+        to_core[2 * step - 1].wait_recv()
+        add_place(-step, 1 - core)
+        to_core[2 * step].wait_recv()
+        add_place(step, 1 - core)
+
+    def rows_of(half):
+        return pl.ds(pl.multiple_of(half * count, count), count)
+
+    def share(turn, half):
+        at = rows_of(half)
+        part_send[at, :] = total[1 - tp, at, :].astype(jnp.bfloat16)
+        return send(part_send.at[at], part_recv.at[at], x_ssem.at[turn], x_rsem.at[turn], across)
+
+    shares = [share(0, near)]
+    to_right[3].wait_recv()
+    to_left[3].wait_recv()
+    to_core.append(pass_on(at_place(4), core_ssem.at[7], core_rsem.at[7], beside))
+    mine, theirs = ring_ctx(at_place(4), core), ring_ctx(at_place(4), 1 - core)
+    add(mine, 1 - tp)
+    to_core[7].wait_recv()
+    add(theirs, 1 - tp)
+    shares.append(share(1, 1 - near))
+    add(mine, tp)
+    add(theirs, tp)
+    for turn, half in enumerate((near, 1 - near)):
+        at = rows_of(half)
+        shares[turn].wait_recv()
+        proj_ref[at, :] = (total[tp, at, :] + part_recv[at, :].astype(jnp.float32)).astype(jnp.bfloat16)
+    for copy in shares + to_core + to_right + to_left:
+        copy.wait_send()
+
+
+def gather_multiply(tokens, w_in):
+    rows, cols = w_in.shape
+    count, depth = tokens.shape
+    seq_len, width = 2 * count, cols // 2
+    bf16 = functools.partial(pltpu.VMEM, dtype=jnp.bfloat16)
+    dma = pltpu.SemaphoreType.DMA
+    vmem = pl.BlockSpec(memory_space=pltpu.VMEM)
+    return pl.pallas_call(
+        gather_kernel,
+        out_shape=jax.ShapeDtypeStruct((seq_len, width), jnp.bfloat16),
+        in_specs=[vmem, pl.BlockSpec(memory_space=pl.ANY)],
+        out_specs=vmem,
+        scratch_shapes=[
+            bf16((rows, cols)),
+            bf16((16, count, depth)),
+            pltpu.VMEM((2, seq_len, width), jnp.float32),
+            bf16((seq_len, width)),
+            bf16((seq_len, width)),
+            dma((2,)), dma, dma, dma((8,)), dma((8,)),
+            dma((4,)), dma((4,)), dma((4,)), dma((4,)), dma((2,)), dma((2,)),
+        ],
+        compiler_params=pltpu.CompilerParams(
+            collective_id=0, has_side_effects=True, vmem_limit_bytes=56 * 1024 * 1024
+        ),
+        cost_estimate=pl.CostEstimate(
+            flops=2 * rows * cols * seq_len, bytes_accessed=2 * rows * cols, transcendentals=0
+        ),
+        name="gather_multiply",
+    )(tokens, w_in)
 
 
 def mix_kernel(seq_len, chans, modes, chunks, proj_ref, spread_ref, taps_ref, rate_ref, res_ref,
@@ -427,33 +563,15 @@
     )(projected, spread, taps, per_row(li_rate), per_row(li_residue), cotangent)
 
 
-def fast_shards(n_ctx, n_tp, tokens, w_in, short_taps, li_residue, li_rate, cotangent):
-    pairs = swap_pairs(n_ctx, n_tp)
-    tp = lax.axis_index("tp")
-    rows, cols = w_in.shape
-    half_cols = cols // 2
-    piece = lax.ppermute(tokens, ("ctx", "tp"), pairs)
-    features = lax.all_gather(piece, "ctx", axis=1, tiled=True)
-
-    def partial(side):
-        weights = lax.dynamic_slice_in_dim(w_in, side * half_cols, half_cols, 1)
-        return jnp.concatenate(
-            [
-                jnp.dot(features[:, i * rows:(i + 1) * rows], weights, preferred_element_type=jnp.float32)
-                for i in range(n_tp)
-            ],
-            axis=0,
-        )
-
-    other = lax.ppermute(partial(1 - tp).astype(jnp.bfloat16), "tp", [(0, 1), (1, 0)])
-    projected = (partial(tp) + other.astype(jnp.float32)).astype(jnp.bfloat16)
+def fast_shards(tokens, w_in, short_taps, li_residue, li_rate, cotangent):
+    projected = gather_multiply(tokens, w_in)
     mixed, grad = mix(projected, short_taps, li_residue, li_rate, cotangent)
     return mixed, multiply_scatter(w_in, grad)
 
 
 def solution(mesh):
     n_ctx, n_tp = mesh.shape["ctx"], mesh.shape["tp"]
-    body = functools.partial(fast_shards, n_ctx, n_tp) if (n_ctx, n_tp) == (16, 2) else shards
+    body = fast_shards if (n_ctx, n_tp) == (16, 2) else shards
     in_specs = (
         P("tp", "ctx"),
         P("tp", "ctx"),

time: 301 us -> 244 us (0.81)
  waiting for transfers between devices: 124 us -> 0 us
  Pallas kernels: 123 us -> 234 us
  matrix products: 27.6 us -> 0 us
  between operations: 14.2 us -> 0.71 us
  starting transfers between devices: 5.13 us -> 0 us
    pallas_call x0 -> x1, Pallas kernels: none -> 108 us  [gather_multiply(): pl.pallas_call(gather_kernel, out_shape=jax.ShapeDtypeStruct((seq_len, wi...]
    all_gather x1 -> x0, waiting for transfers between devices: 78.4 us -> none  [fast_shards(): features = lax.all_gather(piece, 'ctx', axis=1, tiled=True)]
    ppermute x2 -> x0, waiting for transfers between devices: 45.3 us -> none  [the longest x1 24.3 us: fast_shards(): piece = lax.ppermute(tokens, ('ctx', 'tp'), pairs)]
    dot_general x4 -> x0, matrix products: 27.6 us -> none  [partial(): jnp.dot(features[:, i * rows:(i + 1) * rows], weights, preferred_element_...]
    ppermute x2 -> x0, starting transfers between devices: 5.09 us -> none  [the longest x1 4.47 us: fast_shards(): piece = lax.ppermute(tokens, ('ctx', 'tp'), pairs)]
  transfers between devices with their start and end apart: 3 -> 0, of which waited for: 3 -> 0; matrix products, arithmetic and copies ran while one was open for 5% -> 0% of each run, Pallas kernels for 0% -> 0%
where the time goes in v3:
time: 244 us; the launch traced here: 243 us
  Pallas kernels  234 us (96%)
  local copies, waits for them, and re-layouts  7.09 us (3%)
    pallas_call x1, Pallas kernels, multiply_scatter(): pl.pallas_call(scatter_kernel, out_shape=jax.ShapeDtypeStruct((block, blo...  110 us
    pallas_call x1, Pallas kernels, gather_multiply(): pl.pallas_call(gather_kernel, out_shape=jax.ShapeDtypeStruct((seq_len, wi...  108 us
    pallas_call x1, Pallas kernels, mix(): pl.pallas_call(functools.partial(mix_kernel, seq_len, chans, modes, chunk...  16.3 us

profile of v3, /device:TPU:2, one launch (start us, length us, event | category | flops | bytes accessed | tf_op | source)
XLA Modules:
  0.0 242.6 jit_solution(5133658602112834772)
XLA Ops:
  0.6 0.7 tile.23
  1.4 0.7 tile.20
  2.2 1.0 reshape.73
  3.2 0.1 copy.9
  3.3 0.4 fusion.spread_ref
  3.7 0.0 copy-start
  3.8 108.1 %gather_multiply.1.proj_ref = bf16[1024,768]{1,0:T(8,128)(2,1)} custom-call(bf16[512,512]{1,0:T(8,128)(2,1)} %tokens_ref.1, bf16[4096,1536]{1,0:T(8,128)(2,1)} %w_hbm.3), custom_call_target="tpu_custom_call" | custom-call | flops 12884901888 | bytes 12582912 | tf_op jit(solution)/shard_map/gather_multiply/pallas_call | solution.py:390
  111.9 0.0 copy-done
  111.9 0.0 copy-start.2
  111.9 1.4 copy-done.2
  113.3 16.3 %mix.1 = (bf16[256,1024]{1,0:T(8,128)(2,1)}, bf16[1024,768]{1,0:T(8,128)(2,1)S(1)}) custom-call(bf16[1024,768]{1,0:T(8,128)(2,1)S(1)} %copy-done.2, bf16[768,768]{1,0:T(8,128)(2,1)S(1)} %fusion.spread_ref, f32[3,768]{1,0:T(4,128)S(1)} %bitcast.9, f32[16,8,128]{2,1,0:T(8,128)S(1)} %bitcast.7, f32[16,8,128]{2,1,0:T(8,128)S(1)} %bitcast.8, ...), custom_call_target="tpu_custom_call" | custom-call | flops 20000000000 | bytes 4718592 | tf_op jit(solution)/shard_map/mix/pallas_call | solution.py:540
  129.6 0.0 copy-start.1
  129.6 1.2 copy-done.1
  130.8 110.0 %multiply_scatter.1 = bf16[512,512]{1,0:T(8,128)(2,1)} custom-call(bf16[1024,768]{1,0:T(8,128)(2,1)} %copy-done.1, bf16[4096,1536]{1,0:T(8,128)(2,1)} %w_hbm.3), custom_call_target="tpu_custom_call" | custom-call | flops 12884901888 | bytes 12582912 | tf_op jit(solution)/shard_map/multiply_scatter/pallas_call | solution.py:238
  240.8 1.9 copy.12
  (4 shorter events, 0.1 us)
Async XLA Ops:
  3.7 108.2 %copy-start = (bf16[256,1024]{1,0:T(8,128)(2,1)S(1)}, bf16[256,1024]{1,0:T(8,128)(2,1)}, u32[]{:S(2)}) copy-start(bf16[256,1024]{1,0:T(8,128)(2,1)} %cot_ref.1) | copy-start | bytes 1572868
  111.9 1.4 copy-start.2
  129.6 1.2 copy-start.1

commit v4 on v3

--- a/solution.py
+++ b/solution.py
@@ -182,49 +182,67 @@
     to_core[0].wait_recv()
     right_send[0, top, :] = mine(0, top).astype(jnp.bfloat16)
     left_send[0, bottom, :] = mine(0, bottom).astype(jnp.bfloat16)
-    to_right = [send(right_send.at[0, top], right_recv.at[0, top], r_ssem.at[0], r_rsem.at[0], right)]
-    to_left = [send(left_send.at[0, bottom], left_recv.at[0, bottom], l_ssem.at[0], l_rsem.at[0], left)]
+    to_right = {(0, 0): send(right_send.at[0, top], right_recv.at[0, top], r_ssem.at[0, 0], r_rsem.at[0, 0], right)}
+    to_left = {(0, 1): send(left_send.at[0, bottom], left_recv.at[0, bottom], l_ssem.at[0, 1], l_rsem.at[0, 1], left)}
     for k in (1, 2, 3, 4):
         both(k)
+    sides = (top, bottom)
+
+    def relay(step, side, k, sent, out, got, ssem, rsem, where):
+        rows = sides[side]
+        value = mine(k, rows)
+        if (step - 1, side) in sent:
+            sent[step - 1, side].wait_recv()
+            value = value + got[step - 1, rows, :].astype(jnp.float32)
+        out[step, rows, :] = value.astype(jnp.bfloat16)
+        sent[step, side] = send(
+            out.at[step, rows], got.at[step, rows], ssem.at[step, side], rsem.at[step, side], where
+        )
+
     for step in (1, 2, 3):
-        k = 2 * step - 1
-        to_core[k].wait_recv()
-        to_right[step - 1].wait_recv()
-        if step == 1:
-            right_send[1, top, :] = (mine(k, top) + right_recv[0, top, :].astype(jnp.float32)).astype(jnp.bfloat16)
-            right_send[1, bottom, :] = mine(k, bottom).astype(jnp.bfloat16)
-        else:
-            right_send[step] = (mine(k, whole) + right_recv[step - 1].astype(jnp.float32)).astype(jnp.bfloat16)
-        to_right.append(send(right_send.at[step], right_recv.at[step], r_ssem.at[step], r_rsem.at[step], right))
-        k += 1
-        to_core[k].wait_recv()
-        to_left[step - 1].wait_recv()
-        if step == 1:
-            left_send[1, top, :] = mine(k, top).astype(jnp.bfloat16)
-            left_send[1, bottom, :] = (mine(k, bottom) + left_recv[0, bottom, :].astype(jnp.float32)).astype(jnp.bfloat16)
-        else:
-            left_send[step] = (mine(k, whole) + left_recv[step - 1].astype(jnp.float32)).astype(jnp.bfloat16)
-        to_left.append(send(left_send.at[step], left_recv.at[step], l_ssem.at[step], l_rsem.at[step], left))
+        to_core[2 * step - 1].wait_recv()
+        to_core[2 * step].wait_recv()
+        for side in range(2):
+            relay(step, 1 - side, 2 * step - 1, to_right, right_send, right_recv, r_ssem, r_rsem, right)
+            relay(step, side, 2 * step, to_left, left_send, left_recv, l_ssem, l_rsem, left)
         if step == 1:
             for k in (5, 6, 7):
                 both(k)
     to_core[7].wait_recv()
-    to_right[3].wait_recv()
-    to_left[3].wait_recv()
-    total = mine(7, whole) + right_recv[3].astype(jnp.float32) + left_recv[3].astype(jnp.float32)
-    last[...] = total.astype(jnp.bfloat16)
+
+    def ending(side):
+        rows = sides[side]
+        return pltpu.make_async_remote_copy(
+            src_ref=last.at[rows], dst_ref=landed.at[rows], send_sem=end_ssem.at[side],
+            recv_sem=end_rsem.at[side], device_id=owner, device_id_type=MESH,
+        )
+
+    to_right[3, 1].wait_recv()
+    to_left[3, 0].wait_recv()
+    for side in range(2):
+        rows = sides[side]
+        if side == 0:
+            to_right[3, 0].wait_recv()
+        else:
+            to_left[3, 1].wait_recv()
+        total = mine(7, rows) + right_recv[3, rows, :].astype(jnp.float32) + left_recv[3, rows, :].astype(jnp.float32)
+        last[rows, :] = total.astype(jnp.bfloat16)
+
+        @pl.when(near != tp)
+        def _():
+            ending(side).start()
 
     @pl.when(near != tp)
     def _():
-        end = send(last, landed, end_ssem, end_rsem, owner)
-        end.wait()
-        out_ref[...] = landed[...]
+        for side in range(2):
+            ending(side).wait()
+            out_ref[sides[side], :] = landed[sides[side], :]
 
     @pl.when(near == tp)
     def _():
         out_ref[...] = last[...]
 
-    for copy in shares + to_core + to_right + to_left:
+    for copy in shares + to_core + list(to_right.values()) + list(to_left.values()):
         copy.wait_send()
 
 
@@ -253,7 +271,7 @@
             bf16((block, block)),
             bf16((block, block)),
             dma((2,)), dma((2,)), dma((2,)), dma((8,)), dma((8,)),
-            dma((4,)), dma((4,)), dma((4,)), dma((4,)), dma, dma,
+            dma((4, 2)), dma((4, 2)), dma((4, 2)), dma((4, 2)), dma((2,)), dma((2,)),
         ],
         compiler_params=pltpu.CompilerParams(
             collective_id=1, has_side_effects=True, vmem_limit_bytes=56 * 1024 * 1024
@@ -287,19 +305,28 @@
         copy.start()
         return copy
 
-    def pass_on(place_of, ssem, rsem, where, rows=None):
+    top, bottom = slice(0, count // 2), slice(count // 2, count)
+    sides = (top, bottom)
+
+    def pass_on(place_of, ssem, rsem, where, side=None):
         piece = ring_ctx(place_of, core)
-        ref = pieces.at[piece] if rows is None else pieces.at[piece, rows]
+        ref = pieces.at[piece] if side is None else pieces.at[piece, sides[side]]
         return send(ref, ref, ssem, rsem, where)
 
     def at_place(turn):
         return (place + turn + 8) % 8
 
+    def swap(side):
+        return pltpu.make_async_remote_copy(
+            src_ref=tokens_ref.at[sides[side]], dst_ref=pieces.at[owner[0], sides[side]],
+            send_sem=swap_ssem.at[side], recv_sem=swap_rsem.at[side], device_id=owner, device_id_type=MESH,
+        )
+
     @pl.when(near != tp)
     def _():
-        swap = send(tokens_ref, pieces.at[owner[0]], swap_ssem, swap_rsem, owner)
+        swap(0).start()
+        swap(1).start()
         total[...] = jnp.zeros_like(total)
-        swap.wait()
 
     @pl.when(near == tp)
     def _():
@@ -307,8 +334,14 @@
         keep.start()
         keep.wait()
 
-    to_right = [pass_on(place, r_ssem.at[0], r_rsem.at[0], right)]
-    to_left = [pass_on(place, l_ssem.at[0], l_rsem.at[0], left)]
+    to_right, to_left = {}, {}
+    for side in range(2):
+        @pl.when(near != tp)
+        def _():
+            swap(side).wait()
+
+        to_right[0, side] = pass_on(place, r_ssem.at[0, side], r_rsem.at[0, side], right, side)
+        to_left[0, side] = pass_on(place, l_ssem.at[0, side], l_rsem.at[0, side], left, side)
     to_core = [pass_on(place, core_ssem.at[0], core_rsem.at[0], beside)]
 
     @pl.when(near == tp)
@@ -335,13 +368,19 @@
             add(ring_ctx(at_place(turn), whose), side)
 
     add_place(0, core)
-    top, bottom = slice(0, count // 2), slice(count // 2, count)
     for step in (1, 2, 3):
-        to_right[step - 1].wait_recv()
-        to_right.append(pass_on(at_place(-step), r_ssem.at[step], r_rsem.at[step], right, top if step == 3 else None))
+        for side in range(2):
+            to_right[step - 1, side].wait_recv()
+            if step < 3 or side == 0:
+                to_right[step, side] = pass_on(
+                    at_place(-step), r_ssem.at[step, side], r_rsem.at[step, side], right, side
+                )
+            to_left[step - 1, side].wait_recv()
+            if step < 3 or side == 1:
+                to_left[step, side] = pass_on(
+                    at_place(step), l_ssem.at[step, side], l_rsem.at[step, side], left, side
+                )
         to_core.append(pass_on(at_place(-step), core_ssem.at[2 * step - 1], core_rsem.at[2 * step - 1], beside))
-        to_left[step - 1].wait_recv()
-        to_left.append(pass_on(at_place(step), l_ssem.at[step], l_rsem.at[step], left, bottom if step == 3 else None))
         to_core.append(pass_on(at_place(step), core_ssem.at[2 * step], core_rsem.at[2 * step], beside))
         add_place(-step, core)
         add_place(step, core)
@@ -362,8 +401,8 @@
         return send(part_send.at[at], part_recv.at[at], x_ssem.at[turn], x_rsem.at[turn], across)
 
     shares = [share(0, near)]
-    to_right[3].wait_recv()
-    to_left[3].wait_recv()
+    to_right[3, 0].wait_recv()
+    to_left[3, 1].wait_recv()
     to_core.append(pass_on(at_place(4), core_ssem.at[7], core_rsem.at[7], beside))
     mine, theirs = ring_ctx(at_place(4), core), ring_ctx(at_place(4), 1 - core)
     add(mine, 1 - tp)
@@ -376,7 +415,7 @@
         at = rows_of(half)
         shares[turn].wait_recv()
         proj_ref[at, :] = (total[tp, at, :] + part_recv[at, :].astype(jnp.float32)).astype(jnp.bfloat16)
-    for copy in shares + to_core + to_right + to_left:
+    for copy in shares + to_core + list(to_right.values()) + list(to_left.values()):
         copy.wait_send()
 
 
@@ -398,8 +437,8 @@
             pltpu.VMEM((2, seq_len, width), jnp.float32),
             bf16((seq_len, width)),
             bf16((seq_len, width)),
-            dma((2,)), dma, dma, dma((8,)), dma((8,)),
-            dma((4,)), dma((4,)), dma((4,)), dma((4,)), dma((2,)), dma((2,)),
+            dma((2,)), dma((2,)), dma((2,)), dma((8,)), dma((8,)),
+            dma((4, 2)), dma((4, 2)), dma((4, 2)), dma((4, 2)), dma((2,)), dma((2,)),
         ],
         compiler_params=pltpu.CompilerParams(
             collective_id=0, has_side_effects=True, vmem_limit_bytes=56 * 1024 * 1024

time: 244 us -> 236 us (0.967)
  Pallas kernels: 234 us -> 228 us
    pallas_call x1, Pallas kernels: 108 us -> 101 us  [gather_multiply(): pl.pallas_call(gather_kernel, out_shape=jax.ShapeDtypeStruct((seq_len, wi...]
where the time goes in v4:
time: 236 us
  Pallas kernels  228 us (97%)
  local copies, waits for them, and re-layouts  7.09 us (3%)
    pallas_call x1, Pallas kernels, multiply_scatter(): pl.pallas_call(scatter_kernel, out_shape=jax.ShapeDtypeStruct((block, blo...  111 us
    pallas_call x1, Pallas kernels, gather_multiply(): pl.pallas_call(gather_kernel, out_shape=jax.ShapeDtypeStruct((seq_len, wi...  101 us
    pallas_call x1, Pallas kernels, mix(): pl.pallas_call(functools.partial(mix_kernel, seq_len, chans, modes, chunk...  16.3 us

profile of v4, /device:TPU:2, one launch (start us, length us, event | category | flops | bytes accessed | tf_op | source)
XLA Modules:
  0.0 235.7 jit_solution(13065760659223724458)
XLA Ops:
  0.6 0.7 tile.23
  1.4 0.7 tile.20
  2.2 1.0 reshape.73
  3.2 0.1 copy.9
  3.3 0.4 fusion.spread_ref
  3.7 0.0 copy-start
  3.8 100.6 %gather_multiply.1.proj_ref = bf16[1024,768]{1,0:T(8,128)(2,1)} custom-call(bf16[512,512]{1,0:T(8,128)(2,1)} %tokens_ref.1, bf16[4096,1536]{1,0:T(8,128)(2,1)} %w_hbm.3), custom_call_target="tpu_custom_call" | custom-call | flops 12884901888 | bytes 12582912 | tf_op jit(solution)/shard_map/gather_multiply/pallas_call | solution.py:429
  104.4 0.0 copy-done
  104.4 0.0 copy-start.2
  104.4 1.4 copy-done.2
  105.8 16.3 %mix.1 = (bf16[256,1024]{1,0:T(8,128)(2,1)}, bf16[1024,768]{1,0:T(8,128)(2,1)S(1)}) custom-call(bf16[1024,768]{1,0:T(8,128)(2,1)S(1)} %copy-done.2, bf16[768,768]{1,0:T(8,128)(2,1)S(1)} %fusion.spread_ref, f32[3,768]{1,0:T(4,128)S(1)} %bitcast.9, f32[16,8,128]{2,1,0:T(8,128)S(1)} %bitcast.7, f32[16,8,128]{2,1,0:T(8,128)S(1)} %bitcast.8, ...), custom_call_target="tpu_custom_call" | custom-call | flops 20000000000 | bytes 4718592 | tf_op jit(solution)/shard_map/mix/pallas_call | solution.py:579
  122.1 0.0 copy-start.1
  122.1 1.2 copy-done.1
  123.2 110.6 %multiply_scatter.1 = bf16[512,512]{1,0:T(8,128)(2,1)} custom-call(bf16[1024,768]{1,0:T(8,128)(2,1)} %copy-done.1, bf16[4096,1536]{1,0:T(8,128)(2,1)} %w_hbm.3), custom_call_target="tpu_custom_call" | custom-call | flops 12884901888 | bytes 12582912 | tf_op jit(solution)/shard_map/multiply_scatter/pallas_call | solution.py:256
  233.9 1.9 copy.12
  (4 shorter events, 0.1 us)
Async XLA Ops:
  3.7 100.6 %copy-start = (bf16[256,1024]{1,0:T(8,128)(2,1)S(1)}, bf16[256,1024]{1,0:T(8,128)(2,1)}, u32[]{:S(2)}) copy-start(bf16[256,1024]{1,0:T(8,128)(2,1)} %cot_ref.1) | copy-start | bytes 1572868
  104.4 1.4 copy-start.2
  122.1 1.2 copy-start.1
